TPU v7x, 128 devices: a whole 4x4x4 slice. The times are simulated.
128 devices in a mesh: dp: 64 (over z, y, x), mem: 2 (over core).
Axes of the slice: x: 4, y: 4, z: 4, core: 2. Of those that a mesh axis runs over, the one named last changes fastest.
Arguments:
- tokens: bfloat16 [64, 192, 1024], P('dp', 'mem'), may hold values from -16 to 16
- memory: bfloat16 [2, 64, 48, 1024], P(None, 'dp', 'mem'), may hold values from -6 to 6
- lengths: int32 [64], replicated, may hold values from 24 to 192, as said below
- segments: int32 [64, 192], P('dp'), may hold values from 0 to 2, as said below
- key_mask: int32 [64, 24], P('dp', 'mem'), may hold values from 0 to 1, as said below
- w_self_qkv: bfloat16 [1024, 3072], replicated, may hold values from -0.1875 to 0.1875
- w_self_out: bfloat16 [1024, 1024], replicated, may hold values from -1 to 1
- w_cross_q: bfloat16 [1024, 1024], replicated, may hold values from -0.1875 to 0.1875
- w_cross_kv: bfloat16 [1024, 2048], replicated, may hold values from -0.1875 to 0.1875
- w_cross_out: bfloat16 [1024, 1024], replicated, may hold values from -1 to 1
- w_up: bfloat16 [1024, 4096], replicated, may hold values from -0.1875 to 0.1875
- w_down: bfloat16 [4096, 1024], replicated, may hold values from -0.09375 to 0.09375
- norm_gains: float32 [4, 1024], replicated, may hold values from 0.5 to 1.5
- norm_biases: float32 [4, 1024], replicated, may hold values from -1.2 to 1.2
- readout: bfloat16 [1024, 25088], P(None, ('dp', 'mem')), may hold values from -0.375 to 0.375
Outputs:
- loss: float32 [64], P('dp')
- layer_out: bfloat16 [2, 64, 192, 1024], P(None, 'dp', 'mem')
- tokens_grad: float32 [64, 192, 1024], P('dp', 'mem')
- memory_grad: float32 [2, 64, 48, 1024], P(None, 'dp', 'mem')
- grad_self_qkv: float32 [1024, 3072], P(('dp', 'mem'))
- grad_self_out: float32 [1024, 1024], P(('dp', 'mem'))
- grad_cross_q: float32 [1024, 1024], P(('dp', 'mem'))
- grad_cross_kv: float32 [1024, 2048], P(('dp', 'mem'))
- grad_cross_out: float32 [1024, 1024], P(('dp', 'mem'))
- grad_up: float32 [1024, 4096], P(('dp', 'mem'))
- grad_down: float32 [4096, 1024], P(('dp', 'mem'))
- grad_gains: float32 [4, 1024], P(None, ('dp', 'mem'))
- grad_biases: float32 [4, 1024], P(None, ('dp', 'mem'))
Inputs may be any that keep to these rules, and one draw needn't show every extreme that they name: `lengths`: one page has exactly 192 tokens and another exactly 24. Along each page the ids never fall; segments 0, 1 and 2 are all present, and segment 1 holds positions 95 and 96. `key_mask`: entries 0 and 12 of every page are 1, entry 1 is 0.
All inputs are finite; a program needn't handle non-finite values.
Results may differ from a plain program's by a relative error of at most 0.033.
Values may be sent and summed in bfloat16 or wider, within the bound.
No kernel may reach another device: no remote copies, remote signals or barrier semaphores. Data moves between devices by JAX's collectives and lax.ppermute only.
A program may use at most 256 MiB of HBM per device.

v0:
```python
from functools import partial

import jax
import jax.numpy as jnp
from jax import lax
from jax.sharding import PartitionSpec as P

HEAD = 64


epsilon = 1e-05
masked_score = -1e30


def from_behind(block, axis, distance):
    devices = range(lax.axis_size(axis))
    route = [(i - distance, i) for i in devices if i - distance in devices]
    return lax.ppermute(block, axis, route)


def joined(part, axis, combine):
    gathered = jax.tree.map(lambda a: lax.all_gather(a, axis), part)

    def take(source):
        return jax.tree.map(lambda a: lax.dynamic_index_in_dim(a, source, 0, False), gathered)

    return lax.fori_loop(
        1, lax.axis_size(axis), lambda source, state: combine(state, take(source)), take(0)
    )


def product(left, right):
    return jnp.dot(left, right, preferred_element_type=jnp.float32)


def product_left(left, right):
    return lax.dot_general(
        left, right, (((0,), (0,)), ((), ())), preferred_element_type=jnp.float32
    )


def product_right(left, right):
    return lax.dot_general(
        left, right, (((1,), (1,)), ((), ())), preferred_element_type=jnp.float32
    )


def norm_forward(values, gain, bias):
    centre = values - jnp.mean(values, -1, keepdims=True)
    inverse = lax.rsqrt(jnp.mean(centre * centre, -1, keepdims=True) + epsilon)
    normed = centre * inverse
    return (normed * gain + bias, normed, inverse)


def norm_backward(upstream, normed, inverse, gain):
    scaled = upstream * gain
    back = inverse * (
        scaled
        - jnp.mean(scaled, -1, keepdims=True)
        - normed * jnp.mean(scaled * normed, -1, keepdims=True)
    )
    return (back, jnp.sum(upstream * normed, 0), jnp.sum(upstream, 0))


def combine_parts(earlier, later):
    top_value = jnp.maximum(earlier[0], later[0])
    return (
        top_value,
        earlier[1] * jnp.exp(earlier[0] - top_value) + later[1] * jnp.exp(later[0] - top_value),
    )


def combine_views(earlier, later):
    top_first = jnp.maximum(earlier[0], later[0])
    early_first = jnp.exp(earlier[0] - top_first)
    late_first = jnp.exp(later[0] - top_first)
    top_second = jnp.maximum(earlier[3], later[3])
    early_second = jnp.exp(earlier[3] - top_second)
    late_second = jnp.exp(later[3] - top_second)
    return (
        top_first,
        earlier[1] * early_first + later[1] * late_first,
        earlier[2] * early_first + later[2] * late_first,
        top_second,
        earlier[4] * early_second + later[4] * late_second,
    )


def self_scores(query_heads, key_heads, allowed, scale):
    scores = (
        jnp.einsum("qhd,khd->hqk", query_heads, key_heads, preferred_element_type=jnp.float32)
        * scale
    )
    return jnp.where(allowed[None], scores, masked_score)


def cross_scores_of(query_heads, key_cross, keep_keys, scale):
    scores = (
        jnp.einsum("qhd,vkhd->vhqk", query_heads, key_cross, preferred_element_type=jnp.float32)
        * scale
    )
    return jnp.where(keep_keys, scores, masked_score)


def on_device(
    tokens,
    memory,
    lengths,
    segments,
    key_mask,
    w_self_qkv,
    w_self_out,
    w_cross_q,
    w_cross_kv,
    w_cross_out,
    w_up,
    w_down,
    norm_gains,
    norm_biases,
    readout,
):
    tok_rows = tokens.shape[1]
    width = tokens.shape[2]
    heads = width // HEAD
    scale = HEAD ** (-0.5)
    page_len = tok_rows * lax.axis_size("mem")
    half_index = lax.axis_index("mem")
    page_index = lax.axis_index("dp")
    inputs = tokens[0].astype(jnp.float32)
    page_segments = segments[0]
    positions = jnp.arange(tok_rows) + half_index * tok_rows
    key_positions = jnp.concatenate([positions - tok_rows, positions])
    key_segments = page_segments[jnp.clip(key_positions, 0, page_len - 1)]
    query_segments = page_segments[positions]
    self_allowed = (
        (key_positions[None, :] <= positions[:, None])
        & (key_positions[None, :] >= 0)
        & (key_segments[None, :] == query_segments[:, None])
    )
    normed_one, norm_one, inverse_one = norm_forward(inputs, norm_gains[0], norm_biases[0])
    normed_one_low = normed_one.astype(jnp.bfloat16)
    joined_low = product(normed_one_low, w_self_qkv).astype(jnp.bfloat16)
    query_self = joined_low[:, :width].reshape(tok_rows, heads, HEAD)
    pairs_own = joined_low[:, width:]
    pairs_prev = from_behind(pairs_own, "mem", 1)
    pairs_all = jnp.concatenate([pairs_prev, pairs_own], 0)
    key_self = pairs_all[:, :width].reshape(2 * tok_rows, heads, HEAD)
    value_self = pairs_all[:, width:].reshape(2 * tok_rows, heads, HEAD)
    scores = self_scores(query_self, key_self, self_allowed, scale)
    score_top = jnp.max(scores, -1, keepdims=True)
    self_lse = score_top + jnp.log(jnp.sum(jnp.exp(scores - score_top), -1, keepdims=True))
    self_probs = jnp.exp(scores - self_lse).astype(jnp.bfloat16)
    attn_self = (
        jnp.einsum("hqk,khd->qhd", self_probs, value_self, preferred_element_type=jnp.float32)
        .reshape(tok_rows, width)
        .astype(jnp.bfloat16)
    )
    hidden_one = inputs + product(attn_self, w_self_out)
    normed_two, norm_two, inverse_two = norm_forward(hidden_one, norm_gains[1], norm_biases[1])
    normed_two_low = normed_two.astype(jnp.bfloat16)
    query_cross = product(normed_two_low, w_cross_q).astype(jnp.bfloat16)
    query_page = lax.all_gather(query_cross, "mem", axis=0, tiled=True)
    query_heads = query_page.reshape(page_len, heads, HEAD)
    patches = memory.shape[2]
    memory_rows = memory[:, 0].reshape(2 * patches, width)
    pairs_cross = (
        product(memory_rows, w_cross_kv).astype(jnp.bfloat16).reshape(2, patches, 2 * width)
    )
    key_cross = pairs_cross[:, :, :width].reshape(2, patches, heads, HEAD)
    value_cross = pairs_cross[:, :, width:].reshape(2, patches, heads, HEAD)
    keep_keys = jnp.repeat(key_mask[0], 2) == 1
    cross_scores = cross_scores_of(query_heads, key_cross, keep_keys, scale)
    part_top = jnp.max(cross_scores, -1)
    part_total = jnp.sum(jnp.exp(cross_scores - part_top[..., None]), -1)
    merged_top, merged_total = joined((part_top, part_total), "mem", combine_parts)
    cross_lse = merged_top + jnp.log(merged_total)
    cross_probs = jnp.exp(cross_scores - cross_lse[..., None]).astype(jnp.bfloat16)
    cross_part = jnp.einsum(
        "vhqk,vkhd->qvhd", cross_probs, value_cross, preferred_element_type=jnp.float32
    ).reshape(page_len, 2, width)
    attn_cross = lax.psum_scatter(cross_part, "mem", scatter_dimension=0, tiled=True).astype(
        jnp.bfloat16
    )
    attn_cross_flat = attn_cross.reshape(2 * tok_rows, width)
    flat_two = (
        hidden_one[:, None, :] + product(attn_cross_flat, w_cross_out).reshape(tok_rows, 2, width)
    ).reshape(2 * tok_rows, width)
    normed_three, norm_three, inverse_three = norm_forward(flat_two, norm_gains[2], norm_biases[2])
    normed_three_low = normed_three.astype(jnp.bfloat16)
    up_values = product(normed_three_low, w_up)
    active_low = jax.nn.gelu(up_values, approximate=False).astype(jnp.bfloat16)
    hidden_three = flat_two + product(active_low, w_down)
    layer_out = jnp.transpose(hidden_three.reshape(tok_rows, 2, width), (1, 0, 2))[:, None].astype(
        jnp.bfloat16
    )
    final_norm, norm_four, inverse_four = norm_forward(hidden_three, norm_gains[3], norm_biases[3])
    final_low = final_norm.astype(jnp.bfloat16).reshape(tok_rows, 2, width)
    count = jnp.sum(lengths).astype(jnp.float32)
    page_length = lengths[page_index]
    readout_half = lax.all_gather(readout, "dp", axis=1, tiled=True)
    final_page = lax.all_gather(final_low, "mem", axis=0, tiled=True)
    logits = jnp.einsum("tvd,dc->tvc", final_page, readout_half, preferred_element_type=jnp.float32)
    first = logits[:, 0]
    second = logits[:, 1]
    first_top = jnp.max(first, -1)
    first_exp = jnp.exp(first - first_top[:, None])
    second_top = jnp.max(second, -1)
    partial_stats = (
        first_top,
        jnp.sum(first_exp, -1),
        jnp.sum(first_exp * (first - second), -1),
        second_top,
        jnp.sum(jnp.exp(second - second_top[:, None]), -1),
    )
    merged = joined(partial_stats, "mem", combine_views)
    first_lse = merged[0] + jnp.log(merged[1])
    second_lse = merged[3] + jnp.log(merged[4])
    cross_mean = merged[2] / merged[1]
    divergence = cross_mean - first_lse + second_lse
    valid_rows = jnp.arange(page_len) < page_length
    row_weight = valid_rows.astype(jnp.float32) / count
    loss = (jnp.sum(jnp.where(valid_rows, divergence, 0.0)) / count).reshape(1)
    first_prob = jnp.exp(first - first_lse[:, None])
    second_prob = jnp.exp(second - second_lse[:, None])
    grad_first = row_weight[:, None] * first_prob * (first - second - cross_mean[:, None])
    grad_second = row_weight[:, None] * (second_prob - first_prob)
    grad_logits = jnp.stack([grad_first, grad_second], 1).astype(jnp.bfloat16)
    grad_final = lax.psum_scatter(
        jnp.einsum("tvc,dc->tvd", grad_logits, readout_half, preferred_element_type=jnp.float32),
        "mem",
        scatter_dimension=0,
        tiled=True,
    )
    grad_three, gain_four, bias_four = norm_backward(
        grad_final.reshape(2 * tok_rows, width), norm_four, inverse_four, norm_gains[3]
    )
    grad_three_low = grad_three.astype(jnp.bfloat16)
    weight_down = product_left(active_low, grad_three_low)
    grad_active = product_right(grad_three_low, w_down)
    unused_value, gelu_back = jax.vjp(partial(jax.nn.gelu, approximate=False), up_values)
    grad_up_low = gelu_back(grad_active)[0].astype(jnp.bfloat16)
    weight_up = product_left(normed_three_low, grad_up_low)
    grad_norm_three, gain_three, bias_three = norm_backward(
        product_right(grad_up_low, w_up), norm_three, inverse_three, norm_gains[2]
    )
    grad_two = grad_three + grad_norm_three
    grad_branch_low = grad_two.astype(jnp.bfloat16)
    weight_cross_out = product_left(attn_cross_flat, grad_branch_low)
    grad_attn_low = (
        product_right(grad_branch_low, w_cross_out).astype(jnp.bfloat16).reshape(tok_rows, 2, width)
    )
    grad_attn_page = lax.all_gather(grad_attn_low, "mem", axis=0, tiled=True)
    grad_heads = grad_attn_page.reshape(page_len, 2, heads, HEAD)
    cross_again = cross_scores_of(query_heads, key_cross, keep_keys, scale)
    cross_prob_wide = jnp.exp(cross_again - cross_lse[..., None])
    grad_probs = jnp.einsum(
        "qvhd,vkhd->vhqk", grad_heads, value_cross, preferred_element_type=jnp.float32
    )
    delta_part = jnp.sum(cross_prob_wide * grad_probs, -1)
    delta_all = lax.psum(delta_part, "mem")
    grad_scores = (cross_prob_wide * (grad_probs - delta_all[..., None])).astype(jnp.bfloat16)
    grad_query_part = (
        jnp.einsum("vhqk,vkhd->qhd", grad_scores, key_cross, preferred_element_type=jnp.float32)
        * scale
    )
    grad_query = lax.psum_scatter(
        grad_query_part.reshape(page_len, width), "mem", scatter_dimension=0, tiled=True
    ).astype(jnp.bfloat16)
    grad_key = (
        jnp.einsum("vhqk,qhd->vkhd", grad_scores, query_heads, preferred_element_type=jnp.float32)
        * scale
    )
    grad_value = jnp.einsum(
        "vhqk,qvhd->vkhd", cross_probs, grad_heads, preferred_element_type=jnp.float32
    )
    grad_pairs_low = (
        jnp.concatenate(
            [grad_key.reshape(2, patches, width), grad_value.reshape(2, patches, width)], -1
        )
        .astype(jnp.bfloat16)
        .reshape(2 * patches, 2 * width)
    )
    weight_cross_kv = product_left(memory_rows, grad_pairs_low)
    memory_grad = product_right(grad_pairs_low, w_cross_kv).reshape(2, 1, patches, width)
    weight_cross_q = product_left(normed_two_low, grad_query)
    grad_norm_two, gain_two, bias_two = norm_backward(
        product_right(grad_query, w_cross_q), norm_two, inverse_two, norm_gains[1]
    )
    grad_one = jnp.sum(grad_two.reshape(tok_rows, 2, width), 1) + grad_norm_two
    grad_self_low = grad_one.astype(jnp.bfloat16)
    weight_self_out = product_left(attn_self, grad_self_low)
    grad_self_heads = (
        product_right(grad_self_low, w_self_out).astype(jnp.bfloat16).reshape(tok_rows, heads, HEAD)
    )
    self_prob_wide = jnp.exp(self_scores(query_self, key_self, self_allowed, scale) - self_lse)
    grad_probs_self = jnp.einsum(
        "qhd,khd->hqk", grad_self_heads, value_self, preferred_element_type=jnp.float32
    )
    delta_self = jnp.sum(self_prob_wide * grad_probs_self, -1, keepdims=True)
    grad_scores_self = (self_prob_wide * (grad_probs_self - delta_self)).astype(jnp.bfloat16)
    grad_query_self = (
        jnp.einsum("hqk,khd->qhd", grad_scores_self, key_self, preferred_element_type=jnp.float32)
        * scale
    )
    grad_key_self = (
        jnp.einsum("hqk,qhd->khd", grad_scores_self, query_self, preferred_element_type=jnp.float32)
        * scale
    )
    grad_value_self = jnp.einsum(
        "hqk,qhd->khd", self_probs, grad_self_heads, preferred_element_type=jnp.float32
    )
    grad_pairs_self = jnp.concatenate(
        [grad_key_self.reshape(2 * tok_rows, width), grad_value_self.reshape(2 * tok_rows, width)],
        -1,
    )
    returned = from_behind(grad_pairs_self[:tok_rows], "mem", -1)
    grad_pairs_own = grad_pairs_self[tok_rows:] + returned
    grad_joined_low = jnp.concatenate(
        [grad_query_self.reshape(tok_rows, width), grad_pairs_own], -1
    ).astype(jnp.bfloat16)
    weight_self_qkv = product_left(normed_one_low, grad_joined_low)
    grad_norm_one, gain_one, bias_one = norm_backward(
        product_right(grad_joined_low, w_self_qkv), norm_one, inverse_one, norm_gains[0]
    )
    tokens_grad = (grad_one + grad_norm_one)[None]
    gain_grads = jnp.stack([gain_one, gain_two, gain_three, gain_four])
    bias_grads = jnp.stack([bias_one, bias_two, bias_three, bias_four])
    scattered = (
        lax.psum_scatter(weight_self_qkv, ("dp", "mem"), scatter_dimension=0, tiled=True),
        lax.psum_scatter(weight_self_out, ("dp", "mem"), scatter_dimension=0, tiled=True),
        lax.psum_scatter(weight_cross_q, ("dp", "mem"), scatter_dimension=0, tiled=True),
        lax.psum_scatter(weight_cross_kv, ("dp", "mem"), scatter_dimension=0, tiled=True),
        lax.psum_scatter(weight_cross_out, ("dp", "mem"), scatter_dimension=0, tiled=True),
        lax.psum_scatter(weight_up, ("dp", "mem"), scatter_dimension=0, tiled=True),
        lax.psum_scatter(weight_down, ("dp", "mem"), scatter_dimension=0, tiled=True),
        lax.psum_scatter(gain_grads, ("dp", "mem"), scatter_dimension=1, tiled=True),
        lax.psum_scatter(bias_grads, ("dp", "mem"), scatter_dimension=1, tiled=True),
    )
    return (
        loss,
        layer_out,
        tokens_grad,
        memory_grad,
        scattered[0],
        scattered[1],
        scattered[2],
        scattered[3],
        scattered[4],
        scattered[5],
        scattered[6],
        scattered[7],
        scattered[8],
    )


def solution(mesh):
    in_specs = (
        P("dp", "mem", None),
        P(None, "dp", "mem", None),
        P(),
        P("dp", None),
        P("dp", "mem"),
        P(),
        P(),
        P(),
        P(),
        P(),
        P(),
        P(),
        P(),
        P(),
        P(None, ("dp", "mem")),
    )
    out_specs = (
        P("dp"),
        P(None, "dp", "mem", None),
        P("dp", "mem", None),
        P(None, "dp", "mem", None),
        P(("dp", "mem"), None),
        P(("dp", "mem"), None),
        P(("dp", "mem"), None),
        P(("dp", "mem"), None),
        P(("dp", "mem"), None),
        P(("dp", "mem"), None),
        P(("dp", "mem"), None),
        P(None, ("dp", "mem")),
        P(None, ("dp", "mem")),
    )
    return jax.shard_map(
        on_device, mesh=mesh, in_specs=in_specs, out_specs=out_specs, check_vma=False
    )
```

profile of v0, /device:TPU:0, one launch (start us, length us, event | category | flops | bytes accessed | tf_op | source)
XLA Modules:
  0.0 4469.6 jit_solution(115704269108879922)
XLA Ops:
  12.1 4.2 convolution_convert_fusion
  19.6 3.1 convolution_convert_fusion.1
  49.7 3.9 copy.120
  53.6 8.6 all-reduce.11
  67.4 2.5 reshape.570
  74.7 14.1 multiply_convert_fusion.2
  88.8 6.1 fusion.128
  99.9 2.9 all_gather.59
  102.8 46.2 %all-gather.10.cloned.1.call-done = bf16[64,196,1024]{2,1,0:T(8,128)(2,1)} async-done(((bf16[1,196,1024]{2,1,0:T(8,128)(2,1)}), bf16[64,196,1024]{2,1,0:T(8,128)(2,1)}) %all-gather.10.cloned.1.call-update) | async-done | bytes 25690128 | tf_op jit(solution)/shard_map/all_gather | solution.py:200
  149.0 31.5 reshape.663
  180.4 21.6 fusion.129
  202.0 7.5 slice_reduce_fusion.1
  209.5 9.2 fusion.5
  221.0 3.9 all-reduce.9
  227.0 12.7 multiply_convert_fusion.1
  239.7 18.8 fusion
  258.8 11.2 reduce-scatter.16.cloned.1.call-done
  270.0 2.7 copy.127
  272.7 2.6 reshape.573
  281.1 2.7 subtract_multiply_fusion
  283.8 9.2 add_convert_fusion
  293.0 7.7 multiply_reduce_fusion.2
  305.5 6.4 all_gather.71
  311.9 3.2 copy.129
  317.5 3.4 psum.7
  329.7 4.0 fusion.74
  334.0 2.5 reshape.574
  336.5 2.8 reduce_sum.325
  342.0 3.1 multiply_reduce_fusion.10
  346.7 2.6 fusion.89
  350.2 3.4 fusion.85
  357.9 4.5 convolution_bitcast_fusion
  362.4 9.2 copy.153
  375.2 3.0 fusion.63
  379.7 2.6 multiply_reduce_fusion
  396.9 7.3 fusion.58
  405.4 9.6 fusion.114
  416.1 9.5 fusion.77
  429.2 4.4 fusion.29
  433.7 5.7 fusion.54
  439.5 70.1 %all-reduce.8 = (f32[4,1024]{1,0:T(4,128)S(1)}, f32[4,1024]{1,0:T(4,128)S(1)}) all-reduce(f32[4,1024]{1,0:T(4,128)S(1)} %pad_maximum_fusion.5, f32[4,1024]{1,0:T(4,128)S(1)} %pad_maximum_fusion.6), channel_id=19, replica_groups=mesh['dp'=64,'mem'=2] {'dp','mem'}, use_global_device_ids=true, to_apply=%region_45.46.clone | all-reduce | flops 8192 | bytes 65536
  512.9 474.6 %reduce-scatter.24.cloned.1.call-done = f32[8,1024]{1,0:T(8,128)} async-done(((f32[1024,1024]{1,0:T(8,128)}), f32[8,1024]{1,0:T(8,128)}) %reduce-scatter.24.cloned.1.call-update) | async-done | bytes 32784 | tf_op jit(solution)/shard_map/reduce_scatter | solution.py:333
  987.4 639.5 %reduce-scatter.20.cloned.1.call-done = f32[8,1024]{1,0:T(8,128)} async-done(((f32[1024,1024]{1,0:T(8,128)}), f32[8,1024]{1,0:T(8,128)}) %reduce-scatter.20.cloned.1.call-update) | async-done | bytes 32784 | tf_op jit(solution)/shard_map/reduce_scatter | solution.py:330
  1627.0 639.1 %reduce-scatter.22.cloned.1.call-done = f32[8,1024]{1,0:T(8,128)} async-done(((f32[1024,1024]{1,0:T(8,128)}), f32[8,1024]{1,0:T(8,128)}) %reduce-scatter.22.cloned.1.call-update) | async-done | bytes 32784 | tf_op jit(solution)/shard_map/reduce_scatter | solution.py:331
  2266.0 647.0 %reduce-scatter.32.cloned.1.call-done = f32[8,2048]{1,0:T(8,128)} async-done(((f32[1024,2048]{1,0:T(8,128)}), f32[8,2048]{1,0:T(8,128)}) %reduce-scatter.32.cloned.1.call-update) | async-done | bytes 65552
  2913.0 220.8 %reduce-scatter.18.cloned.1.call-done = f32[8,3072]{1,0:T(8,128)} async-done(((f32[1024,3072]{1,0:T(8,128)}), f32[8,3072]{1,0:T(8,128)}) %reduce-scatter.18.cloned.1.call-update) | async-done | bytes 98320 | tf_op jit(solution)/shard_map/reduce_scatter | solution.py:329
  3133.8 665.7 %reduce-scatter.26.cloned.1.call-done = f32[8,4096]{1,0:T(8,128)} async-done(((f32[1024,4096]{1,0:T(8,128)}), f32[8,4096]{1,0:T(8,128)}) %reduce-scatter.26.cloned.1.call-update) | async-done | bytes 131088 | tf_op jit(solution)/shard_map/reduce_scatter | solution.py:334
  3799.5 661.6 %reduce-scatter.28.cloned.1.call-done = f32[32,1024]{1,0:T(8,128)} async-done(((f32[4096,1024]{1,0:T(8,128)}), f32[32,1024]{1,0:T(8,128)}) %reduce-scatter.28.cloned.1.call-update) | async-done | bytes 131088 | tf_op jit(solution)/shard_map/reduce_scatter | solution.py:335
  (306 shorter events, 111.6 us)
Async XLA Ops:
  7.2 57.1 %copy-start = (bf16[1024,1024]{1,0:T(8,128)(2,1)S(1)}, bf16[1024,1024]{1,0:T(8,128)(2,1)}, u32[]{:S(2)}) copy-start(bf16[1024,1024]{1,0:T(8,128)(2,1)} %param.24) | copy-start | bytes 6291460
  7.2 141.8 %all-gather.10.cloned.1.call-start = ((), (), s32[]{:S(2)}) async-start(), calls=%async_computation.16 | async-start | bytes 26624000 | tf_op jit(solution)/shard_map/all_gather | solution.py:200
  7.9 262.1 %reduce-scatter.16.cloned.1.call-start = ((), (), s32[]{:S(2)}) async-start(), calls=%async_computation.9 | async-start | bytes 2359296 | tf_op jit(solution)/shard_map/reduce_scatter | solution.py:228
  9.0 7.2 copy-start.60
  10.2 6.0 copy-start.66
  11.1 27.6 copy-start.56
  11.1 63.5 %copy-start.50 = (f32[1,1024]{1,0:T(1,128)}, f32[1,1024]{1,0:T(1,128)S(1)}, u32[]{:S(2)}) copy-start(f32[1,1024]{1,0:T(1,128)S(1)} %get-tuple-element.168) | copy-start | bytes 12292
  12.0 26.7 copy-start.54
  12.1 6.3 copy-start.75
  12.1 7.6 copy-start.44
  16.3 7.6 copy-start.1
  16.3 15.6 collective-permute-start
  19.6 8.0 copy-start.76
  19.6 8.9 copy-start.74
  23.8 12.3 copy-start.28
  38.7 9.2 copy-start.34
  47.9 273.0 %copy-start.42 = (f32[2,16,192]{2,0,1:T(2,128)}, f32[2,16,192]{2,0,1:T(2,128)S(1)}, u32[]{:S(2)}) copy-start(f32[2,16,192]{2,0,1:T(2,128)S(1)} %copy.117) | copy-start | bytes 73732
  74.7 226.1 %copy-start.58 = (f32[192]{0:T(256)}, f32[192]{0:T(256)S(1)}, u32[]{:S(2)}) copy-start(f32[192]{0:T(256)S(1)} %div.73) | copy-start | bytes 2308
  74.7 14.2 copy-start.10
  88.8 6.2 copy-start.32
  209.5 17.5 copy-start.71
  258.6 81.6 %reduce-scatter.30.cloned.1.call-start = ((), (), s32[]{:S(2)}) async-start(), calls=%async_computation.17 | async-start | bytes 1179648
  283.8 17.0 copy-start.13
  283.8 9.3 copy-start.11
  293.0 7.7 copy-start.41
  327.8 659.7 %reduce-scatter.24.cloned.1.call-start = ((), (), s32[]{:S(2)}) async-start(), calls=%async_computation.13 | async-start | bytes 4227072 | tf_op jit(solution)/shard_map/reduce_scatter | solution.py:333
  333.7 8.4 copy-start.55
  333.7 8.4 copy-start.69
  333.7 1293.3 %reduce-scatter.20.cloned.1.call-start = ((), (), s32[]{:S(2)}) async-start(), calls=%async_computation.11 | async-start | bytes 4227072 | tf_op jit(solution)/shard_map/reduce_scatter | solution.py:330
  336.5 10.2 copy-start.27
  349.3 1916.7 %reduce-scatter.22.cloned.1.call-start = ((), (), s32[]{:S(2)}) async-start(), calls=%async_computation.12 | async-start | bytes 4227072 | tf_op jit(solution)/shard_map/reduce_scatter | solution.py:331
  353.7 2559.3 %reduce-scatter.32.cloned.1.call-start = ((), (), s32[]{:S(2)}) async-start(), calls=%async_computation.18 | async-start | bytes 8454144
  356.1 6.3 copy-start.35
  371.6 2762.2 %reduce-scatter.18.cloned.1.call-start = ((), (), s32[]{:S(2)}) async-start(), calls=%async_computation.10 | async-start | bytes 12681216 | tf_op jit(solution)/shard_map/reduce_scatter | solution.py:329
  387.4 9.5 copy-start.7
  387.4 9.5 copy-start.47
  387.4 9.5 copy-start.53
  387.4 9.5 copy-start.61
  387.4 9.5 copy-start.67
  389.4 5.4 collective-permute-start.1
  404.3 3395.3 %reduce-scatter.26.cloned.1.call-start = ((), (), s32[]{:S(2)}) async-start(), calls=%async_computation.14 | async-start | bytes 16908288 | tf_op jit(solution)/shard_map/reduce_scatter | solution.py:334
  415.0 4046.1 %reduce-scatter.28.cloned.1.call-start = ((), (), s32[]{:S(2)}) async-start(), calls=%async_computation.15 | async-start | bytes 16908288 | tf_op jit(solution)/shard_map/reduce_scatter | solution.py:335
  433.6 5.8 copy-start.63
  433.6 5.8 copy-start.65
  433.6 5.8 copy-start.73
  433.6 5.8 copy-start.62
  433.6 5.8 copy-start.64
  433.6 5.8 copy-start.72
  (41 other events, 93.3 us)
Sparse Core Ops, SparseCore 0:
  10.8 138.1 all-gather.9
  258.7 11.2 reduce-scatter.15
  327.9 12.2 reduce-scatter.29
  343.0 644.4 reduce-scatter.23
  990.3 636.5 reduce-scatter.19
  1629.8 636.2 reduce-scatter.21
  2269.1 643.8 reduce-scatter.31
  2918.6 215.1 reduce-scatter.17
  3136.8 662.7 reduce-scatter.25
  3802.3 658.7 reduce-scatter.27
where the time goes:
time: 4480 us; the launch traced here: 4470 us
  waiting for transfers between devices  4010 us (90%)
  matrix products  166 us (4%)
  local copies, waits for them, and re-layouts  112 us (2%)
  blocking collectives  101 us (2%)
  other arithmetic  59.3 us (1%)
    reduce_scatter x1, waiting for transfers between devices, on_device(): lax.psum_scatter(weight_up, ('dp', 'mem'), scatter_dimension=0, tiled=True)  666 us
    reduce_scatter x1, waiting for transfers between devices, on_device(): lax.psum_scatter(weight_down, ('dp', 'mem'), scatter_dimension=0, tiled=T...  662 us
    unnamed x12, waiting for transfers between devices  649 us
    reduce_scatter x1, waiting for transfers between devices, on_device(): lax.psum_scatter(weight_self_out, ('dp', 'mem'), scatter_dimension=0, til...  640 us
    reduce_scatter x1, waiting for transfers between devices, on_device(): lax.psum_scatter(weight_cross_q, ('dp', 'mem'), scatter_dimension=0, tile...  639 us
    reduce_scatter x1, waiting for transfers between devices, on_device(): lax.psum_scatter(weight_cross_out, ('dp', 'mem'), scatter_dimension=0, ti...  475 us
    reduce_scatter x1, waiting for transfers between devices, on_device(): lax.psum_scatter(weight_self_qkv, ('dp', 'mem'), scatter_dimension=0, til...  221 us
  transfers between devices with their start and end apart: 12, of which 10 were waited for; matrix products, arithmetic and copies ran while one was open for 4% of the time, Pallas kernels for 0%

commit v1 on v0

v1 whole, which is shorter than its diff:
```python
from functools import partial

import jax
import jax.numpy as jnp
from jax import lax
from jax.experimental import pallas as pl
from jax.experimental.pallas import tpu as pltpu
from jax.sharding import PartitionSpec as P

HEAD = 64
SIDE = 4
CHIPS = SIDE * SIDE * SIDE
TILE = 256
ROWS = 16
LANES = 208


epsilon = 1e-05
masked_score = -1e30
bf16 = jnp.bfloat16
f32 = jnp.float32


def swapped(block):
    return lax.ppermute(block, "mem", [(0, 1), (1, 0)])


def product(left, right):
    return jnp.dot(left, right, preferred_element_type=f32)


def product_right(left, right):
    return lax.dot_general(left, right, (((1,), (1,)), ((), ())), preferred_element_type=f32)


def norm_forward(values, gain, bias):
    centre = values - jnp.mean(values, -1, keepdims=True)
    inverse = lax.rsqrt(jnp.mean(centre * centre, -1, keepdims=True) + epsilon)
    normed = centre * inverse
    return (normed * gain + bias, normed, inverse)


def norm_backward(upstream, normed, inverse, gain):
    scaled = upstream * gain
    back = inverse * (
        scaled
        - jnp.mean(scaled, -1, keepdims=True)
        - normed * jnp.mean(scaled * normed, -1, keepdims=True)
    )
    return (back, jnp.sum(upstream * normed, 0), jnp.sum(upstream, 0))


def combine_views(earlier, later):
    top_first = jnp.maximum(earlier[0], later[0])
    early_first = jnp.exp(earlier[0] - top_first)
    late_first = jnp.exp(later[0] - top_first)
    top_second = jnp.maximum(earlier[3], later[3])
    early_second = jnp.exp(earlier[3] - top_second)
    late_second = jnp.exp(later[3] - top_second)
    return (
        top_first,
        earlier[1] * early_first + later[1] * late_first,
        earlier[2] * early_first + later[2] * late_first,
        top_second,
        earlier[4] * early_second + later[4] * late_second,
    )


def lines(stride, core):
    starts = [d for d in range(CHIPS) if (d // stride) % SIDE == 0]
    return [[2 * (start + stride * k) + core for k in range(SIDE)] for start in starts]


def exchange(block, strides):
    groups = lines(strides[0], 0) + lines(strides[1], 1)
    return lax.all_to_all(block, ("dp", "mem"), 0, 0, axis_index_groups=groups, tiled=True)


def reduced(bucket):
    for strides in ((1, 4), (4, 16), (16, 1)):
        bucket = bucket.reshape((SIDE, -1) + bucket.shape[1:])
        bucket = exchange(bucket, strides)
        total = bucket.astype(f32).sum(0)
        bucket = total.astype(bf16)
    return total[0]


def outer_kernel(shapes, core_ref, *refs):
    n_in = 4 * len(shapes) + 1
    inputs, out_ref, turned = refs[:n_in], refs[n_in], refs[n_in + 1 :]
    extra = inputs[-1]
    step = pl.program_id(0)
    core = core_ref[0]

    def place(chip):
        z, y, x = chip // 16, (chip // 4) % 4, chip % 4
        return jnp.where(core == 0, x * 16 + y * 4 + z, y * 16 + z * 4 + x)

    first = 0
    for i, (groups, columns) in enumerate(shapes):
        left_a, left_b, right_a, right_b = inputs[4 * i : 4 * i + 4]
        tiles = columns // TILE
        depth = left_a.shape[0]
        low, high = first, first + groups * tiles
        first = high

        @pl.when(step == low)
        def _(left_a=left_a, left_b=left_b, to=turned[i], groups=groups, depth=depth):
            wide = left_a.shape[1]
            for start in range(0, wide, 1024):
                both = jnp.concatenate(
                    [left_a[:, start : start + 1024], left_b[:, start : start + 1024]], 0
                )
                flat = both.T
                if groups == 1:
                    to[0, start : start + 1024] = flat
                else:
                    per = ROWS * groups
                    for c in range(1024 // per):
                        chip = start // per + c
                        for g in range(groups):
                            at = c * per + g * ROWS
                            to[g, chip * ROWS : (chip + 1) * ROWS] = flat[at : at + ROWS]

        @pl.when((step >= low) & (step < high))
        def _(right_a=right_a, right_b=right_b, to=turned[i], tiles=tiles, low=low):
            at = step - low
            group = at // tiles
            tile = at - group * tiles
            column = pl.multiple_of(tile * TILE, TILE)
            both = jnp.concatenate(
                [right_a[:, pl.ds(column, TILE)], right_b[:, pl.ds(column, TILE)]], 0
            )
            result = jnp.dot(to[group], both, preferred_element_type=f32).astype(bf16)
            for chip in range(CHIPS):
                out_ref[place(chip)] = result[chip * ROWS : (chip + 1) * ROWS]

    @pl.when(step == first)
    def _():
        for chip in range(CHIPS):
            out_ref[place(chip)] = extra[chip]


def outer_products(core, items, extra):
    shapes, operands, scratch = [], [], []
    total = 0
    for left, left_other, right, right_other in items:
        groups = left.shape[1] // (ROWS * CHIPS)
        shapes.append((groups, right.shape[1]))
        operands += [left, left_other, right, right_other]
        depth = left.shape[0] + left_other.shape[0]
        scratch.append(pltpu.VMEM((groups, ROWS * CHIPS, depth), bf16))
        total += groups * right.shape[1]
    operands.append(extra)
    width = total + TILE
    flops = sum(2 * s[0] * ROWS * CHIPS * s[1] * 384 for s in shapes)
    return pl.pallas_call(
        partial(outer_kernel, tuple(shapes)),
        out_shape=jax.ShapeDtypeStruct((CHIPS, ROWS, width), bf16),
        grid_spec=pltpu.PrefetchScalarGridSpec(
            num_scalar_prefetch=1,
            grid=(width // TILE,),
            in_specs=[pl.BlockSpec(memory_space=pltpu.VMEM) for _ in operands],
            out_specs=pl.BlockSpec((CHIPS, ROWS, TILE), lambda i, core: (0, 0, i)),
            scratch_shapes=scratch,
        ),
        compiler_params=pltpu.CompilerParams(vmem_limit_bytes=40 * 1024 * 1024),
        cost_estimate=pl.CostEstimate(
            flops=flops, bytes_accessed=CHIPS * ROWS * width * 2, transcendentals=0
        ),
    )(core.reshape(1), *operands)


def norm_vectors(vectors):
    spread = vectors.reshape(8, CHIPS, ROWS).transpose(1, 0, 2).reshape(CHIPS, 1, 128)
    return jnp.pad(spread.astype(bf16), ((0, 0), (0, ROWS - 1), (0, TILE - 128)))


def on_device(
    tokens,
    memory,
    lengths,
    segments,
    key_mask,
    w_self_qkv,
    w_self_out,
    w_cross_q,
    w_cross_kv,
    w_cross_out,
    w_up,
    w_down,
    norm_gains,
    norm_biases,
    readout,
):
    tok_rows = tokens.shape[1]
    width = tokens.shape[2]
    heads = width // HEAD
    scale = HEAD ** (-0.5)
    page_len = 2 * tok_rows
    half = lax.axis_index("mem")
    page_index = lax.axis_index("dp")
    patches = 2 * memory.shape[2]

    vocab_dev = readout.shape[1]
    readout_turned = jnp.pad(readout.T, ((0, LANES - vocab_dev), (0, 0)))
    readout_half = lax.all_gather(readout_turned, "dp", axis=0, tiled=True)

    tokens_page = lax.all_gather(tokens[0], "mem", axis=0, tiled=True)
    memory_page = lax.all_gather(memory[:, 0], "mem", axis=1, tiled=True)
    memory_rows = memory_page.reshape(2 * patches, width)
    mask_page = lax.all_gather(
        key_mask[0].astype(f32), "mem", axis=0, tiled=True
    )
    keep_keys = jnp.repeat(mask_page, 2) == 1

    def own_half(full, axis):
        size = full.shape[axis] // 2
        return lax.dynamic_slice_in_dim(full, half * size, size, axis)

    def other_half(full, axis):
        size = full.shape[axis] // 2
        return lax.dynamic_slice_in_dim(full, (1 - half) * size, size, axis)

    inputs = tokens[0].astype(f32)
    page_segments = segments[0]
    positions = jnp.arange(tok_rows) + half * tok_rows
    key_positions = jnp.arange(page_len)
    query_segments = own_half(page_segments, 0)
    self_allowed = (key_positions[None, :] <= positions[:, None]) & (
        page_segments[None, :] == query_segments[:, None]
    )
    unused, norm_one, inverse_one = norm_forward(inputs, norm_gains[0], norm_biases[0])
    normed_page = norm_forward(tokens_page.astype(f32), norm_gains[0], norm_biases[0])[0]
    normed_page_low = normed_page.astype(bf16)
    normed_one_low = own_half(normed_page_low, 0)
    query_self = product(normed_one_low, w_self_qkv[:, :width]).astype(bf16)
    query_self = query_self.reshape(tok_rows, heads, HEAD)
    pairs_self = product(normed_page_low, w_self_qkv[:, width:]).astype(bf16)
    key_self = pairs_self[:, :width].reshape(page_len, heads, HEAD)
    value_self = pairs_self[:, width:].reshape(page_len, heads, HEAD)
    scores = jnp.einsum("qhd,khd->hqk", query_self, key_self, preferred_element_type=f32) * scale
    scores = jnp.where(self_allowed[None], scores, masked_score)
    score_top = jnp.max(scores, -1, keepdims=True)
    score_exp = jnp.exp(scores - score_top)
    self_probs = score_exp / jnp.sum(score_exp, -1, keepdims=True)
    self_probs_low = self_probs.astype(bf16)
    attn_self = (
        jnp.einsum("hqk,khd->qhd", self_probs_low, value_self, preferred_element_type=f32)
        .reshape(tok_rows, width)
        .astype(bf16)
    )
    attn_self_other = swapped(attn_self)
    hidden_one = inputs + product(attn_self, w_self_out)

    normed_two, norm_two, inverse_two = norm_forward(hidden_one, norm_gains[1], norm_biases[1])
    normed_two_low = normed_two.astype(bf16)
    normed_two_other = swapped(normed_two_low)
    query_cross = product(normed_two_low, w_cross_q).astype(bf16).reshape(tok_rows, heads, HEAD)
    pairs_cross = product(memory_rows, w_cross_kv).astype(bf16).reshape(2, patches, 2 * width)
    key_cross = pairs_cross[:, :, :width].reshape(2, patches, heads, HEAD)
    value_cross = pairs_cross[:, :, width:].reshape(2, patches, heads, HEAD)
    cross_scores = (
        jnp.einsum("qhd,vkhd->vhqk", query_cross, key_cross, preferred_element_type=f32) * scale
    )
    cross_scores = jnp.where(keep_keys, cross_scores, masked_score)
    cross_exp = jnp.exp(cross_scores - jnp.max(cross_scores, -1, keepdims=True))
    cross_probs = cross_exp / jnp.sum(cross_exp, -1, keepdims=True)
    cross_probs_low = cross_probs.astype(bf16)
    attn_cross = (
        jnp.einsum("vhqk,vkhd->vqhd", cross_probs_low, value_cross, preferred_element_type=f32)
        .reshape(2 * tok_rows, width)
        .astype(bf16)
    )
    attn_cross_other = swapped(attn_cross)
    hidden_two = jnp.concatenate([hidden_one, hidden_one], 0) + product(attn_cross, w_cross_out)

    normed_three, norm_three, inverse_three = norm_forward(
        hidden_two, norm_gains[2], norm_biases[2]
    )
    normed_three_low = normed_three.astype(bf16)
    normed_three_other = swapped(normed_three_low)
    up_values = product(normed_three_low, w_up)
    active_low = jax.nn.gelu(up_values, approximate=False).astype(bf16)
    active_other = swapped(active_low)
    hidden_three = hidden_two + product(active_low, w_down)
    layer_out = hidden_three.reshape(2, 1, tok_rows, width).astype(bf16)

    final_norm, norm_four, inverse_four = norm_forward(hidden_three, norm_gains[3], norm_biases[3])
    final_low = final_norm.astype(bf16).reshape(2, tok_rows, width)
    count = jnp.sum(lengths).astype(f32)
    page_length = lengths[page_index]
    final_page = lax.all_gather(final_low, "mem", axis=1, tiled=True)
    logits = product_right(final_page.reshape(2 * page_len, width), readout_half)
    logits = logits.reshape(2, page_len, -1)
    is_entry = jnp.arange(logits.shape[-1]) % LANES < vocab_dev
    logits = jnp.where(is_entry, logits, masked_score)
    first = logits[0]
    second = logits[1]
    first_top = jnp.max(first, -1)
    first_exp = jnp.exp(first - first_top[:, None])
    second_top = jnp.max(second, -1)
    partial_stats = jnp.stack(
        [
            first_top,
            jnp.sum(first_exp, -1),
            jnp.sum(first_exp * (first - second), -1),
            second_top,
            jnp.sum(jnp.exp(second - second_top[:, None]), -1),
        ]
    )
    all_stats = lax.all_gather(partial_stats, "mem")
    merged = combine_views(tuple(all_stats[0]), tuple(all_stats[1]))
    first_lse = merged[0] + jnp.log(merged[1])
    second_lse = merged[3] + jnp.log(merged[4])
    cross_mean = merged[2] / merged[1]
    divergence = cross_mean - first_lse + second_lse
    valid_rows = jnp.arange(page_len) < page_length
    row_weight = valid_rows.astype(f32) / count
    loss = (jnp.sum(jnp.where(valid_rows, divergence, 0.0)) / count).reshape(1)
    first_prob = jnp.exp(first - first_lse[:, None])
    second_prob = jnp.exp(second - second_lse[:, None])
    grad_first = row_weight[:, None] * first_prob * (first - second - cross_mean[:, None])
    grad_second = row_weight[:, None] * (second_prob - first_prob)
    grad_logits = jnp.stack([grad_first, grad_second], 0).astype(bf16)
    grad_part = product(grad_logits.reshape(2 * page_len, -1), readout_half)
    grad_part = grad_part.reshape(2, page_len, width)
    grad_final = own_half(grad_part, 1) + swapped(other_half(grad_part, 1))

    grad_three, gain_four, bias_four = norm_backward(
        grad_final.reshape(2 * tok_rows, width), norm_four, inverse_four, norm_gains[3]
    )
    grad_three_low = grad_three.astype(bf16)
    grad_three_other = swapped(other_half(grad_three_low, 1))
    grad_active = product_right(grad_three_low, w_down)
    unused_value, gelu_back = jax.vjp(partial(jax.nn.gelu, approximate=False), up_values)
    grad_up_low = gelu_back(grad_active)[0].astype(bf16)
    grad_up_other = swapped(other_half(grad_up_low, 1))
    first_bucket = outer_products(
        half,
        [
            (active_low, active_other, own_half(grad_three_low, 1), grad_three_other),
            (normed_three_low, normed_three_other, own_half(grad_up_low, 1), grad_up_other),
        ],
        jnp.zeros((CHIPS, ROWS, TILE), bf16),
    )
    first_sum = reduced(first_bucket)
    grad_norm_three, gain_three, bias_three = norm_backward(
        product_right(grad_up_low, w_up), norm_three, inverse_three, norm_gains[2]
    )
    grad_two = grad_three + grad_norm_three

    grad_branch_low = grad_two.astype(bf16)
    grad_branch_other = swapped(other_half(grad_branch_low, 1))
    grad_heads = product_right(grad_branch_low, w_cross_out).astype(bf16)
    grad_heads = grad_heads.reshape(2, tok_rows, heads, HEAD)
    grad_probs = jnp.einsum(
        "vqhd,vkhd->vhqk", grad_heads, value_cross, preferred_element_type=f32
    )
    delta = jnp.sum(cross_probs * grad_probs, -1, keepdims=True)
    grad_scores = (cross_probs * (grad_probs - delta)).astype(bf16)
    grad_query = (
        jnp.einsum("vhqk,vkhd->qhd", grad_scores, key_cross, preferred_element_type=f32) * scale
    )
    grad_query = grad_query.reshape(tok_rows, width).astype(bf16)
    grad_query_other = swapped(other_half(grad_query, 1))
    grad_key = (
        jnp.einsum("vhqk,qhd->vkhd", grad_scores, query_cross, preferred_element_type=f32) * scale
    )
    grad_value = jnp.einsum(
        "vhqk,vqhd->vkhd", cross_probs_low, grad_heads, preferred_element_type=f32
    )
    grad_pairs = jnp.concatenate(
        [
            grad_key.reshape(2 * patches, width),
            grad_value.reshape(2 * patches, width),
        ],
        -1,
    )
    grad_pairs_low = (grad_pairs + swapped(grad_pairs)).astype(bf16)
    own_pairs_low = own_half(grad_pairs_low.reshape(2, patches, 2 * width), 1)
    memory_grad = product_right(own_pairs_low.reshape(patches, 2 * width), w_cross_kv)
    memory_grad = memory_grad.reshape(2, 1, patches // 2, width)
    grad_norm_two, gain_two, bias_two = norm_backward(
        product_right(grad_query, w_cross_q), norm_two, inverse_two, norm_gains[1]
    )
    grad_one = grad_two[:tok_rows] + grad_two[tok_rows:] + grad_norm_two

    grad_self_low = grad_one.astype(bf16)
    grad_self_other = swapped(other_half(grad_self_low, 1))
    grad_self_heads = product_right(grad_self_low, w_self_out).astype(bf16)
    grad_self_heads = grad_self_heads.reshape(tok_rows, heads, HEAD)
    grad_probs_self = jnp.einsum(
        "qhd,khd->hqk", grad_self_heads, value_self, preferred_element_type=f32
    )
    delta_self = jnp.sum(self_probs * grad_probs_self, -1, keepdims=True)
    grad_scores_self = (self_probs * (grad_probs_self - delta_self)).astype(bf16)
    grad_query_self = (
        jnp.einsum("hqk,khd->qhd", grad_scores_self, key_self, preferred_element_type=f32) * scale
    )
    grad_query_self = grad_query_self.reshape(tok_rows, width).astype(bf16)
    grad_query_self_other = swapped(other_half(grad_query_self, 1))
    grad_key_self = (
        jnp.einsum("hqk,qhd->khd", grad_scores_self, query_self, preferred_element_type=f32)
        * scale
    )
    grad_value_self = jnp.einsum(
        "hqk,qhd->khd", self_probs_low, grad_self_heads, preferred_element_type=f32
    )
    grad_pairs_self = jnp.concatenate(
        [grad_key_self.reshape(page_len, width), grad_value_self.reshape(page_len, width)], -1
    )
    grad_pairs_self_low = (grad_pairs_self + swapped(grad_pairs_self)).astype(bf16)
    grad_joined_low = jnp.concatenate([grad_query_self, own_half(grad_pairs_self_low, 0)], -1)
    grad_norm_one, gain_one, bias_one = norm_backward(
        product_right(grad_joined_low, w_self_qkv), norm_one, inverse_one, norm_gains[0]
    )
    tokens_grad = (grad_one + grad_norm_one)[None]

    vectors = jnp.stack(
        [gain_one, gain_two, gain_three, gain_four, bias_one, bias_two, bias_three, bias_four]
    )
    normed_one_other = other_half(normed_page_low, 0)
    pairs_here = grad_pairs_self_low.reshape(page_len, 2, width)
    pairs_here = own_half(pairs_here, 2).reshape(page_len, width)
    memory_low = grad_pairs_low.reshape(2 * patches, 2, width)
    memory_low = own_half(memory_low, 2).reshape(2 * patches, width)
    second_bucket = outer_products(
        half,
        [
            (
                normed_one_low,
                normed_one_other,
                jnp.concatenate([own_half(grad_query_self, 1), own_half(pairs_here, 0)], -1),
                jnp.concatenate([grad_query_self_other, other_half(pairs_here, 0)], -1),
            ),
            (attn_self, attn_self_other, own_half(grad_self_low, 1), grad_self_other),
            (normed_two_low, normed_two_other, own_half(grad_query, 1), grad_query_other),
            (memory_rows[:patches], memory_rows[patches:], memory_low[:patches], memory_low[patches:]),
            (attn_cross, attn_cross_other, own_half(grad_branch_low, 1), grad_branch_other),
        ],
        norm_vectors(vectors),
    )
    second_sum = reduced(second_bucket)

    down_width = width // 2 * 4
    down = first_sum[:, :down_width].reshape(ROWS, 2, 2, width // 2)
    down = down.transpose(1, 2, 0, 3).reshape(2, -1)
    up_width = first_sum.shape[1] - down_width - TILE
    up = first_sum[:, down_width : down_width + up_width].reshape(2, -1)
    rest_width = second_sum.shape[1] - TILE
    rest = second_sum[:, :rest_width].reshape(2, -1)
    vector_sum = second_sum[0, rest_width : rest_width + 128]
    mine = jnp.concatenate([down, up, rest], 1)
    keep = lax.dynamic_index_in_dim(mine, half, 0, False)
    give = lax.dynamic_index_in_dim(mine, 1 - half, 0, False)
    come = swapped(jnp.concatenate([give, vector_sum]))
    vector_sum = vector_sum + come[-128:]
    vector_sum = own_half(vector_sum.reshape(8, ROWS), 1)
    come = come[:-128]
    left = jnp.where(half == 0, keep, come)
    right = jnp.where(half == 0, come, keep)

    def sides(at, rows, columns):
        size = rows * columns
        return left[at : at + size].reshape(rows, columns), right[at : at + size].reshape(
            rows, columns
        )

    weight_down = jnp.concatenate(sides(0, 2 * ROWS, width // 2), 1)
    at = down.shape[1]
    weight_up = jnp.concatenate(sides(at, ROWS // 2, up_width), 1)
    at += up.shape[1]
    rest_left, rest_right = sides(at, ROWS // 2, rest_width)

    def columns(start, size):
        return jnp.concatenate(
            [rest_left[:, start : start + size], rest_right[:, start : start + size]], 1
        )

    part = width // 2
    weight_self_qkv = jnp.concatenate([columns(k * part, part) for k in range(3)], 1)
    weight_self_out = columns(3 * part, part)
    weight_cross_q = columns(4 * part, part)
    weight_cross_kv = jnp.concatenate([columns((5 + k) * part, part) for k in range(2)], 1)
    weight_cross_out = columns(7 * part, part)
    return (
        loss,
        layer_out,
        tokens_grad,
        memory_grad,
        weight_self_qkv,
        weight_self_out,
        weight_cross_q,
        weight_cross_kv,
        weight_cross_out,
        weight_up,
        weight_down,
        vector_sum[:4],
        vector_sum[4:],
    )
def solution(mesh):
    in_specs = (
        P("dp", "mem", None),
        P(None, "dp", "mem", None),
        P(),
        P("dp", None),
        P("dp", "mem"),
        P(),
        P(),
        P(),
        P(),
        P(),
        P(),
        P(),
        P(),
        P(),
        P(None, ("dp", "mem")),
    )
    out_specs = (
        P("dp"),
        P(None, "dp", "mem", None),
        P("dp", "mem", None),
        P(None, "dp", "mem", None),
        P(("dp", "mem"), None),
        P(("dp", "mem"), None),
        P(("dp", "mem"), None),
        P(("dp", "mem"), None),
        P(("dp", "mem"), None),
        P(("dp", "mem"), None),
        P(("dp", "mem"), None),
        P(None, ("dp", "mem")),
        P(None, ("dp", "mem")),
    )
    return jax.shard_map(
        on_device, mesh=mesh, in_specs=in_specs, out_specs=out_specs, check_vma=False
    )
```

time: 4480 us -> 547 us (0.12)
  waiting for transfers between devices: 4010 us -> 152 us
  blocking collectives: 101 us -> 11.9 us
    reduce_scatter x7 -> x0, waiting for transfers between devices: 3310 us -> none  [the longest x1 666 us: on_device(): lax.psum_scatter(weight_up, ('dp', 'mem'), scatter_dimension=0, tiled=True)]
    unnamed x12 -> x1, waiting for transfers between devices: 649 us -> 0.02 us
    unnamed x3 -> x1, blocking collectives: 82.6 us -> 2.74 us
    all_to_all x0 -> x6, waiting for transfers between devices: none -> 73.2 us  [exchange(): lax.all_to_all(block, ('dp', 'mem'), 0, 0, axis_index_groups=groups, tile...]
    dot_general x24 -> x15, matrix products: 123 us -> 56.3 us  [the longest x9 45.9 us: product(): return jnp.dot(left, right, preferred_element_type=f32)]
  transfers between devices with their start and end apart: 12 -> 22, of which waited for: 10 -> 5; matrix products, arithmetic and copies ran while one was open for 4% -> 35% of each run, Pallas kernels for 0% -> 4%
where the time goes in v1:
time: 547 us; the launch traced here: 538 us
  waiting for transfers between devices  152 us (28%)
  matrix products  122 us (22%)
  local copies, waits for them, and re-layouts  91.2 us (17%)
  other arithmetic  84.3 us (15%)
  starting transfers between devices  34.7 us (6%)
  Pallas kernels  23.7 us (4%)
  between operations  18.5 us (3%)
  blocking collectives  11.9 us (2%)
    all_gather x1, waiting for transfers between devices, on_device(): readout_half = lax.all_gather(readout_turned, 'dp', axis=0, tiled=True)  77.3 us
    all_to_all x6, waiting for transfers between devices, exchange(): lax.all_to_all(block, ('dp', 'mem'), 0, 0, axis_index_groups=groups, tile...  73.2 us
    dot_general x8, matrix products, product_right(): lax.dot_general(left, right, (((1,), (1,)), ((), ())), preferred_element_...  53.6 us
    dot_general x9, matrix products, product(): return jnp.dot(left, right, preferred_element_type=f32)  45.9 us
    all_to_all x6, starting transfers between devices, exchange(): lax.all_to_all(block, ('dp', 'mem'), 0, 0, axis_index_groups=groups, tile...  30.5 us
    unnamed x162, local copies, waits for them, and re-layouts  25.5 us
    pallas_call x2, Pallas kernels, outer_products(): pl.pallas_call(partial(outer_kernel, tuple(shapes)), out_shape=jax.ShapeD...  23.7 us
    reduce_sum x6, other arithmetic, reduced(): total = bucket.astype(f32).sum(0)  19.8 us
  transfers between devices with their start and end apart: 22, of which 5 were waited for; matrix products, arithmetic and copies ran while one was open for 35% of the time, Pallas kernels for 4%

profile of v1, /device:TPU:0, one launch (start us, length us, event | category | flops | bytes accessed | tf_op | source)
XLA Modules:
  0.0 538.0 jit_solution(12202832272743890398)
XLA Ops:
  11.7 2.2 all-gather.1
  14.0 3.1 convolution_convert_fusion
  21.6 3.3 fusion.28
  27.5 2.2 fusion.44
  30.9 2.7 fusion.128
  33.6 2.2 convolution_convert_fusion.3
  40.4 2.7 all-reduce.2
  49.5 2.1 convert_element_type.179
  56.0 13.0 %multiply_convert_fusion.2 = (bf16[192,4096]{1,0:T(8,128)(2,1)S(1)}, f32[192,4096]{1,0:T(8,128)}, f32[192,4096]{1,0:T(8,128)}) fusion(bf16[192,1024]{1,0:T(8,128)(2,1)} %add_convert_fusion.4.refs_4_, bf16[1024,4096]{1,0:T(8,128)(2,1)} %param.25), kind=kOutput, calls=%fused_computation.31 | convolution fusion | flops 1661730816 | bytes 16646144 | tf_op jit(solution)/shard_map/dot_general | solution.py:29
  72.1 3.0 all_gather.24
  75.1 77.3 %all-gather.7.cloned.1.call-done = bf16[13312,1024]{1,0:T(8,128)(2,1)} async-done(((bf16[208,1024]{1,0:T(8,128)(2,1)}), bf16[13312,1024]{1,0:T(8,128)(2,1)}) %all-gather.7.cloned.1.call-update) | async-done | bytes 27262992 | tf_op jit(solution)/shard_map/all_gather | solution.py:207
  152.5 22.8 %fusion.6 = f32[2,192,13312]{2,1,0:T(8,128)} fusion(bf16[2,192,1024]{2,1,0:T(8,128)(2,1)} %all_gather.24, bf16[13312,1024]{1,0:T(8,128)(2,1)} %all-gather.7.cloned.1.call-done, pred[13312]{0:T(1024)(128)(4,1)S(1)} %fusion.90), kind=kOutput, calls=%fused_computation.6 | convolution fusion | flops 10474094592 | bytes 48509952 | tf_op jit(solution)/shard_map/dot_general | solution.py:33
  175.3 7.8 %slice_reduce_fusion = (f32[192]{0:T(256)S(1)}, f32[192]{0:T(256)S(1)}) fusion(f32[2,192,13312]{2,1,0:T(8,128)} %fusion.6), kind=kLoop, calls=%fused_computation.22 | loop fusion | flops 5111424 | bytes 20448768 | tf_op jit(solution)/shard_map/reduce_max | solution.py:302
  183.1 9.0 %fusion.13 = (f32[192]{0:T(256)S(1)}, f32[192]{0:T(256)S(1)}, f32[192]{0:T(256)S(1)}) fusion(f32[2,192,13312]{2,1,0:T(8,128)} %fusion.6, f32[192]{0:T(256)S(1)} %get-tuple-element.69, f32[192]{0:T(256)S(1)} %get-tuple-element.68), kind=kLoop, calls=%fused_computation.13 | loop fusion | flops 17890752 | bytes 20451072 | tf_op jit(solution)/shard_map/reduce_sum | solution.py:307
  195.2 13.2 %multiply_convert_fusion.1 = (bf16[1,192,13312]{2,1,0:T(8,128)(2,1)}, bf16[1,192,13312]{2,1,0:T(8,128)(2,1)}) fusion(f32[2,192,13312]{2,1,0:T(8,128)} %fusion.6, f32[192]{0:T(256)S(1)} %get-tuple-element.97, f32[192]{0:T(256)S(1)} %get-tuple-element.96, f32[192]{0:T(256)S(1)} %fusion.99, f32[192]{0:T(256)S(1)} %get-tuple-element.98), kind=kLoop, calls=%fused_computation.20 | loop fusion | flops 25559040 | bytes 30673920 | tf_op jit(solution)/shard_map/convert.20
  208.4 19.6 %fusion.2 = f32[2,192,1024]{2,1,0:T(8,128)} fusion(bf16[13312,1024]{1,0:T(8,128)(2,1)} %all-gather.7.cloned.1.call-done, bf16[1,192,13312]{2,1,0:T(8,128)(2,1)} %get-tuple-element.102, bf16[1,192,13312]{2,1,0:T(8,128)(2,1)} %get-tuple-element.101), kind=kOutput, calls=%fused_computation.2 | convolution fusion | flops 10474094592 | bytes 39059456 | tf_op jit(solution)/shard_map/dot_general | solution.py:29
  241.6 2.8 fusion.117
  244.4 8.2 %add_convert_fusion = bf16[192,4096]{1,0:T(8,128)(2,1)S(1)} fusion(f32[192,4096]{1,0:T(8,128)S(1)} %copy-done.67, f32[192,4096]{1,0:T(8,128)} %get-tuple-element.179, bf16[192,1024]{1,0:T(8,128)(2,1)S(1)} %get-tuple-element.92, bf16[4096,1024]{1,0:T(8,128)(2,1)} %param.26), kind=kOutput, calls=%fused_computation.30 | convolution fusion | flops 1621622784 | bytes 16646144 | tf_op jit(solution)/shard_map/dot_general | solution.py:33
  252.6 7.1 %multiply_reduce_fusion.1 = (bf16[1024]{0:T(1024)(128)(2,1)S(1)}, f32[192]{0:T(256)S(1)}, f32[192]{0:T(256)S(1)}, bf16[1024]{0:T(1024)(128)(2,1)}, f32[192,1024]{1,0:T(8,128)S(1)}) fusion(f32[192,1024]{1,0:T(8,128)S(1)} %get-tuple-element.178, f32[192]{0:T(256)S(1)} %add_rsqrt_fusion.1, f32[192]{0:T(256)S(1)} %broadcast_multiply_fusion.5, ...), kind=kOutput, calls=%fused_computation.95 | convolution fusion | flops 1612379648 | bytes 11545600 | tf_op jit(solution)/shard_map/dot_general | solution.py:33
  266.7 2.2 reshape.583
  272.6 14.3 %shard_map.249 = bf16[64,16,4352]{2,1,0:T(8,128)(2,1)} custom-call(s32[1]{0:T(128)} %bitcast.72.core_ref, bf16[192,4096]{1,0:T(8,128)(2,1)S(1)} %copy-done.3, bf16[192,4096]{1,0:T(8,128)(2,1)} %collective-permute-done.3.refs_1_, bf16[192,512]{1,0:T(8,128)(2,1)S(1)} %get-tuple-element.124.refs_2_, bf16[192,512]{1,0:T(8,128)(2,1)S(1)} %collective-permute-done.4.refs_3_, ...), custom_call_target="tpu_custom_call" | custom-call | flops 3221225472 | bytes 8912896 | tf_op jit(solution)/shard_map/pallas_call | solution.py:157
  286.9 6.1 %all-to-all-start = ((bf16[4,16,16,4352]{3,2,1,0:T(8,128)(2,1)}), bf16[4,16,16,4352]{3,2,1,0:T(8,128)(2,1)}, u32[]{:S(2)}, u32[]{:S(2)}) async-start(bf16[4,16,16,4352]{3,2,1,0:T(8,128)(2,1)} %bitcast.259), calls=%async_computation | async-start | bytes 17825792 | tf_op jit(solution)/shard_map/all_to_all | solution.py:76
  294.5 2.6 multiply_reduce_fusion.9
  299.8 3.0 fusion.81
  304.4 2.5 multiply_reduce_fusion
  309.7 2.4 copy.143
  312.1 2.5 pad_maximum_fusion
  327.3 2.4 fusion.42
  342.8 2.2 add_convert_fusion.2
  350.0 2.7 add_convert_fusion.1
  352.6 3.3 reshape.597
  358.1 6.3 %fusion.76 = (bf16[1024]{0:T(1024)(128)(2,1)S(1)}, f32[96]{0:T(128)}, f32[96]{0:T(128)}, bf16[1024]{0:T(1024)(128)(2,1)S(1)}, f32[96,1024]{1,0:T(8,128)}) fusion(bf16[1,96,1024]{2,1,0:T(8,128)(2,1)} %param.15, f32[96]{0:T(128)S(1)} %add_rsqrt_fusion.3, f32[96]{0:T(128)S(1)} %broadcast_multiply_fusion.9, f32[1024]{0:T(1024)S(1)} %bitcast.300, ...), kind=kOutput, calls=%fused_computation.133 | convolution fusion | flops 606140160 | bytes 7480832 | tf_op jit(solution)/shard_map/dot_general | solution.py:33
  364.7 6.9 %reduce_sum.408 = bf16[16,16,4352]{2,1,0:T(8,128)(2,1)} reduce(bf16[4,16,16,4352]{3,2,1,0:T(8,128)(2,1)} %all-to-all-done, bf16[]{:T(256)} %constant.151.clone.1), dimensions={0}, to_apply=%region_31.32 | reduce | flops 3342336 | bytes 11141122 | tf_op jit(solution)/shard_map/reduce_sum | solution.py:83
  371.6 4.6 all-to-all-start.1
  386.7 9.4 %shard_map.250 = bf16[64,16,4352]{2,1,0:T(8,128)(2,1)S(1)} custom-call(s32[1]{0:T(128)} %bitcast.72.core_ref, bf16[96,1024]{1,0:T(8,128)(2,1)S(1)} %copy-done.6, bf16[96,1024]{1,0:T(8,128)(2,1)S(1)} %copy-done.4, bf16[96,1536]{1,0:T(8,128)(2,1)S(1)} %pad_maximum_fusion.1.refs_2_, bf16[96,1536]{1,0:T(8,128)(2,1)S(1)} %pad_maximum_fusion.2.refs_3_, ...), custom_call_target="tpu_custom_call" | custom-call | flops 3221225472 | bytes 8912896 | tf_op jit(solution)/shard_map/pallas_call | solution.py:157
  396.1 3.4 copy-done.1
  399.6 5.7 %all-to-all-start.3 = ((bf16[4,16,16,4352]{3,2,1,0:T(8,128)(2,1)}), bf16[4,16,16,4352]{3,2,1,0:T(8,128)(2,1)}, u32[]{:S(2)}, u32[]{:S(2)}) async-start(bf16[4,16,16,4352]{3,2,1,0:T(8,128)(2,1)} %bitcast.256), calls=%async_computation.3 | async-start | bytes 17825792 | tf_op jit(solution)/shard_map/all_to_all | solution.py:76
  406.0 2.9 reduce_sum.409
  408.9 49.4 %all-to-all-done.3 = bf16[4,16,16,4352]{3,2,1,0:T(8,128)(2,1)} async-done(((bf16[4,16,16,4352]{3,2,1,0:T(8,128)(2,1)}), bf16[4,16,16,4352]{3,2,1,0:T(8,128)(2,1)}, u32[]{:S(2)}, u32[]{:S(2)}) %all-to-all-start.3) | async-done | bytes 8912928 | tf_op jit(solution)/shard_map/all_to_all | solution.py:76
  458.4 4.6 all-to-all-start.2
  463.0 4.2 fusion.47
  467.3 6.9 %reduce_sum.419 = bf16[16,16,4352]{2,1,0:T(8,128)(2,1)} reduce(bf16[4,16,16,4352]{3,2,1,0:T(8,128)(2,1)} %all-to-all-done.3, bf16[]{:T(256)} %constant.151.clone.1), dimensions={0}, to_apply=%region_42.43 | reduce | flops 3342336 | bytes 11141122 | tf_op jit(solution)/shard_map/reduce_sum | solution.py:83
  474.2 4.5 all-to-all-start.4
  479.8 16.2 %all-to-all-done.4 = bf16[4,4,16,4352]{3,2,1,0:T(8,128)(2,1)} async-done(((bf16[4,4,16,4352]{3,2,1,0:T(8,128)(2,1)}), bf16[4,4,16,4352]{3,2,1,0:T(8,128)(2,1)}, u32[]{:S(2)}, u32[]{:S(2)}) %all-to-all-start.4) | async-done | bytes 2228256 | tf_op jit(solution)/shard_map/all_to_all | solution.py:76
  496.0 2.9 reduce_sum.420
  498.9 4.9 all-to-all-start.5
  504.5 7.6 %all-to-all-done.5 = bf16[4,1,16,4352]{3,2,1,0:T(8,128)(2,1)S(1)} async-done(((bf16[4,1,16,4352]{3,2,1,0:T(8,128)(2,1)}), bf16[4,1,16,4352]{3,2,1,0:T(8,128)(2,1)S(1)}, u32[]{:S(2)}, u32[]{:S(2)}) %all-to-all-start.5) | async-done | bytes 557088 | tf_op jit(solution)/shard_map/all_to_all | solution.py:76
  513.7 2.8 fusion.113
  (359 shorter events, 125.4 us)
Async XLA Ops:
  7.2 45.8 %copy-start = (bf16[1024,1024]{1,0:T(8,128)(2,1)S(1)}, bf16[1024,1024]{1,0:T(8,128)(2,1)}, u32[]{:S(2)}) copy-start(bf16[1024,1024]{1,0:T(8,128)(2,1)} %param.24) | copy-start | bytes 6291460
  7.2 145.3 %all-gather.7.cloned.1.call-start = ((), (), s32[]{:S(2)}) async-start(), calls=%async_computation.6 | async-start | bytes 27688960 | tf_op jit(solution)/shard_map/all_gather | solution.py:207
  14.0 6.9 %copy-start.38 = (bf16[2,1,48,1024]{3,2,1,0:T(8,128)(2,1)}, bf16[2,1,48,1024]{3,2,1,0:T(8,128)(2,1)S(1)}, u32[]{:S(2)}) copy-start(bf16[2,1,48,1024]{3,2,1,0:T(8,128)(2,1)S(1)} %all-gather.1) | copy-start | bytes 589828
  14.0 7.3 %copy-start.55 = (f32[4,1024]{1,0:T(4,128)S(1)}, f32[4,1024]{1,0:T(4,128)}, u32[]{:S(2)}) copy-start(f32[4,1024]{1,0:T(4,128)} %param.28) | copy-start | bytes 49156
  14.0 7.3 %copy-start.56 = (f32[4,1024]{1,0:T(4,128)S(1)}, f32[4,1024]{1,0:T(4,128)}, u32[]{:S(2)}) copy-start(f32[4,1024]{1,0:T(4,128)} %param.27) | copy-start | bytes 49156
  27.5 6.2 %copy-start.5 = (bf16[96,1024]{1,0:T(8,128)(2,1)}, bf16[96,1024]{1,0:T(8,128)(2,1)S(1)}, u32[]{:S(2)}) copy-start(bf16[96,1024]{1,0:T(8,128)(2,1)S(1)} %get-tuple-element.122.refs_0_) | copy-start | bytes 589828
  36.0 7.3 %copy-start.50 = (bf16[2,48,1024]{2,1,0:T(8,128)(2,1)S(1)}, bf16[2,48,1024]{2,1,0:T(8,128)(2,1)}, u32[]{:S(2)}) copy-start(bf16[2,48,1024]{2,1,0:T(8,128)(2,1)} %get-tuple-element.125) | copy-start | bytes 589828
  36.5 16.4 %copy-start.16 = (f32[96,1024]{1,0:T(8,128)}, f32[96,1024]{1,0:T(8,128)S(1)}, u32[]{:S(2)}) copy-start(f32[96,1024]{1,0:T(8,128)S(1)} %get-tuple-element.174) | copy-start | bytes 1179652
  45.8 6.5 %copy-start.33 = (f32[2,16,96,48]{2,3,0,1:T(8,128)}, f32[2,16,96,48]{2,3,0,1:T(8,128)S(1)}, u32[]{:S(2)}) copy-start(f32[2,16,96,48]{2,3,0,1:T(8,128)S(1)} %get-tuple-element.176) | copy-start | bytes 1769476
  54.7 197.9 %copy-start.14 = (f32[192,1024]{1,0:T(8,128)}, f32[192,1024]{1,0:T(8,128)S(1)}, u32[]{:S(2)}) copy-start(f32[192,1024]{1,0:T(8,128)S(1)} %get-tuple-element.178) | copy-start | bytes 2359300
  54.8 14.3 %slice-start = ((s8[8388608]{0:T(1024)(128)(4,1)}), s8[4194304]{0:T(1024)(128)(4,1)S(1)}, s32[]{:S(2)}) async-start(s8[8388608]{0:T(1024)(128)(4,1)} %bitcast.330), calls=%async_computation.7 | async-start | bytes 8388608
  56.0 13.1 %slice-start.1 = ((s8[8388608]{0:T(1024)(128)(4,1)}), s8[4194304]{0:T(1024)(128)(4,1)S(1)}, s32[]{:S(2)}) async-start(s8[8388608]{0:T(1024)(128)(4,1)} %bitcast.330), calls=%async_computation.8 | async-start | bytes 8388608
  208.4 22.9 %copy-start.47 = (bf16[16,64,96]{2,1,0:T(8,128)(2,1)S(1)}, bf16[16,64,96]{2,1,0:T(8,128)(2,1)}, u32[]{:S(2)}) copy-start(bf16[16,64,96]{2,1,0:T(8,128)(2,1)} %copy-done.46) | copy-start | bytes 589828
  230.1 7.7 %collective-permute-start = (f32[2,96,1024]{2,1,0:T(8,128)}, f32[2,96,1024]{2,1,0:T(8,128)}, u32[]{:S(2)}, u32[]{:S(2)}) collective-permute-start(f32[2,96,1024]{2,1,0:T(8,128)} %constant_dynamic-slice_fusion.22), channel_id=1, source_target_pairs={{0,1},{1,0},{2,3},{3,2},{4,5},{5,4},{6,7},{7,6},{8,9},{9,8},{10,11... | collective-permute-start | bytes 2359304 | tf_op jit(solution)/shard_map/ppermute | solution.py:25
  230.3 147.8 %collective-permute-start.10 = (bf16[96,1024]{1,0:T(8,128)(2,1)S(1)}, bf16[96,1024]{1,0:T(8,128)(2,1)}, u32[]{:S(2)}, u32[]{:S(2)}) collective-permute-start(bf16[96,1024]{1,0:T(8,128)(2,1)S(1)} %add_convert_fusion.5.refs_8_), channel_id=1, source_target_pairs={{0,1},{1,0},{2,3},{3,2},{4,5},{5,4},{6,7},{7,6},{8,9},{9,8},{10,11... | collective-permute-start | bytes 589832 | tf_op jit(solution)/shard_map/ppermute | solution.py:25
  230.6 41.8 %collective-permute-start.3 = (bf16[192,4096]{1,0:T(8,128)(2,1)}, bf16[192,4096]{1,0:T(8,128)(2,1)}, u32[]{:S(2)}, u32[]{:S(2)}) collective-permute-start(bf16[192,4096]{1,0:T(8,128)(2,1)} %copy-done.2), channel_id=1, source_target_pairs={{0,1},{1,0},{2,3},{3,2},{4,5},{5,4},{6,7},{7,6},{8,9},{9,8},{10,11... | collective-permute-start | bytes 4718600 | tf_op jit(solution)/shard_map/ppermute | solution.py:25
  230.8 41.2 %collective-permute-start.5 = (bf16[192,1024]{1,0:T(8,128)(2,1)}, bf16[192,1024]{1,0:T(8,128)(2,1)}, u32[]{:S(2)}, u32[]{:S(2)}) collective-permute-start(bf16[192,1024]{1,0:T(8,128)(2,1)} %add_convert_fusion.4.refs_4_), channel_id=1, source_target_pairs={{0,1},{1,0},{2,3},{3,2},{4,5},{5,4},{6,7},{7,6},{8,9},{9,8},{10,11... | collective-permute-start | bytes 1179656 | tf_op jit(solution)/shard_map/ppermute | solution.py:25
  233.4 6.1 %copy-start.19 = (f32[192,1024]{1,0:T(8,128)S(1)}, f32[192,1024]{1,0:T(8,128)}, u32[]{:S(2)}) copy-start(f32[192,1024]{1,0:T(8,128)} %copy-done.18) | copy-start | bytes 2359300
  244.4 8.2 %copy-start.41 = (bf16[192,1024]{1,0:T(8,128)(2,1)}, bf16[192,1024]{1,0:T(8,128)(2,1)S(1)}, u32[]{:S(2)}) copy-start(bf16[192,1024]{1,0:T(8,128)(2,1)S(1)} %get-tuple-element.92) | copy-start | bytes 1179652
  260.7 11.9 %collective-permute-start.6 = (bf16[192,2048]{1,0:T(8,128)(2,1)}, bf16[192,2048]{1,0:T(8,128)(2,1)}, u32[]{:S(2)}, u32[]{:S(2)}) collective-permute-start(bf16[192,2048]{1,0:T(8,128)(2,1)} %get-tuple-element.103), channel_id=1, source_target_pairs={{0,1},{1,0},{2,3},{3,2},{4,5},{5,4},{6,7},{7,6},{8,9},{9,8},{10,11... | collective-permute-start | bytes 2359304 | tf_op jit(solution)/shard_map/ppermute | solution.py:25
  270.9 1.7 collective-permute-start.4
  272.1 105.6 %collective-permute-start.8 = (bf16[96,1024]{1,0:T(8,128)(2,1)}, bf16[96,1024]{1,0:T(8,128)(2,1)}, u32[]{:S(2)}, u32[]{:S(2)}) collective-permute-start(bf16[96,1024]{1,0:T(8,128)(2,1)} %copy.167.refs_4_), channel_id=1, source_target_pairs={{0,1},{1,0},{2,3},{3,2},{4,5},{5,4},{6,7},{7,6},{8,9},{9,8},{10,11... | collective-permute-start | bytes 589832 | tf_op jit(solution)/shard_map/ppermute | solution.py:25
  272.4 105.7 %collective-permute-start.12 = (bf16[192,1024]{1,0:T(8,128)(2,1)S(1)}, bf16[192,1024]{1,0:T(8,128)(2,1)}, u32[]{:S(2)}, u32[]{:S(2)}) collective-permute-start(bf16[192,1024]{1,0:T(8,128)(2,1)S(1)} %copy.168.refs_16_), channel_id=1, source_target_pairs={{0,1},{1,0},{2,3},{3,2},{4,5},{5,4},{6,7},{7,6},{8,9},{9,8},{10,11... | collective-permute-start | bytes 1179656 | tf_op jit(solution)/shard_map/ppermute | solution.py:25
  286.9 7.6 %copy-start.17 = (f32[96,1024]{1,0:T(8,128)S(1)}, f32[96,1024]{1,0:T(8,128)}, u32[]{:S(2)}) copy-start(f32[96,1024]{1,0:T(8,128)} %copy-done.16) | copy-start | bytes 1179652
  286.9 77.8 %all-to-all-start = ((bf16[4,16,16,4352]{3,2,1,0:T(8,128)(2,1)}), bf16[4,16,16,4352]{3,2,1,0:T(8,128)(2,1)}, u32[]{:S(2)}, u32[]{:S(2)}) async-start(bf16[4,16,16,4352]{3,2,1,0:T(8,128)(2,1)} %bitcast.259), calls=%async_computation | async-start | bytes 17825792 | tf_op jit(solution)/shard_map/all_to_all | solution.py:76
  314.6 34.8 %collective-permute-start.1 = (f32[192,2048]{1,0:T(8,128)}, f32[192,2048]{1,0:T(8,128)}, u32[]{:S(2)}, u32[]{:S(2)}) collective-permute-start(f32[192,2048]{1,0:T(8,128)} %pad_maximum_fusion), channel_id=1, source_target_pairs={{0,1},{1,0},{2,3},{3,2},{4,5},{5,4},{6,7},{7,6},{8,9},{9,8},{10,11... | collective-permute-start | bytes 4718600 | tf_op jit(solution)/shard_map/ppermute | solution.py:25
  318.7 8.6 %copy-start.63 = (f32[96]{0:T(128)S(1)}, f32[96]{0:T(128)}, u32[]{:S(2)}) copy-start(f32[96]{0:T(128)} %fusion.77) | copy-start | bytes 1156
  321.4 15.7 %copy-start.60 = (bf16[1024]{0:T(1024)(128)(2,1)S(1)}, bf16[1024]{0:T(1024)(128)(2,1)}, u32[]{:S(2)}) copy-start(bf16[1024]{0:T(1024)(128)(2,1)} %get-tuple-element.79) | copy-start | bytes 6148
  327.1 15.4 %collective-permute-start.2 = (f32[96,2048]{1,0:T(8,128)}, f32[96,2048]{1,0:T(8,128)}, u32[]{:S(2)}, u32[]{:S(2)}) collective-permute-start(f32[96,2048]{1,0:T(8,128)} %constant_dynamic-update-slice_fusion), channel_id=1, source_target_pairs={{0,1},{1,0},{2,3},{3,2},{4,5},{5,4},{6,7},{7,6},{8,9},{9,8},{10,11... | collective-permute-start | bytes 2359304 | tf_op jit(solution)/shard_map/ppermute | solution.py:25
  327.3 30.8 %copy-start.58 = (f32[96]{0:T(128)}, f32[96]{0:T(128)S(1)}, u32[]{:S(2)}) copy-start(f32[96]{0:T(128)S(1)} %add_rsqrt_fusion.3) | copy-start | bytes 1156
  342.5 33.9 %collective-permute-start.7 = (bf16[96,512]{1,0:T(8,128)(2,1)}, bf16[96,512]{1,0:T(8,128)(2,1)}, u32[]{:S(2)}, u32[]{:S(2)}) collective-permute-start(bf16[96,512]{1,0:T(8,128)(2,1)} %get-tuple-element.149), channel_id=1, source_target_pairs={{0,1},{1,0},{2,3},{3,2},{4,5},{5,4},{6,7},{7,6},{8,9},{9,8},{10,11... | collective-permute-start | bytes 294920 | tf_op jit(solution)/shard_map/ppermute | solution.py:25
  349.4 8.7 %copy-start.54 = (f32[1,1024]{1,0:T(1,128)S(1)}, f32[1,1024]{1,0:T(1,128)}, u32[]{:S(2)}) copy-start(f32[1,1024]{1,0:T(1,128)} %copy-done.53) | copy-start | bytes 12292
  349.4 28.7 %collective-permute-start.9 = (bf16[96,512]{1,0:T(8,128)(2,1)}, bf16[96,512]{1,0:T(8,128)(2,1)}, u32[]{:S(2)}, u32[]{:S(2)}) collective-permute-start(bf16[96,512]{1,0:T(8,128)(2,1)} %get-tuple-element.147), channel_id=1, source_target_pairs={{0,1},{1,0},{2,3},{3,2},{4,5},{5,4},{6,7},{7,6},{8,9},{9,8},{10,11... | collective-permute-start | bytes 294920 | tf_op jit(solution)/shard_map/ppermute | solution.py:25
  371.6 7.9 %copy-start.4 = (bf16[96,1024]{1,0:T(8,128)(2,1)S(1)}, bf16[96,1024]{1,0:T(8,128)(2,1)}, u32[]{:S(2)}) copy-start(bf16[96,1024]{1,0:T(8,128)(2,1)} %get-tuple-element.121.refs_1_) | copy-start | bytes 589828
  371.6 28.0 %all-to-all-start.1 = ((bf16[4,4,16,4352]{3,2,1,0:T(8,128)(2,1)}), bf16[4,4,16,4352]{3,2,1,0:T(8,128)(2,1)}, u32[]{:S(2)}, u32[]{:S(2)}) async-start(bf16[4,4,16,4352]{3,2,1,0:T(8,128)(2,1)} %bitcast.260), calls=%async_computation.1 | async-start | bytes 4456448 | tf_op jit(solution)/shard_map/all_to_all | solution.py:76
  376.3 3.1 collective-permute-start.13
  377.7 1.7 collective-permute-start.11
  399.6 58.8 %all-to-all-start.3 = ((bf16[4,16,16,4352]{3,2,1,0:T(8,128)(2,1)}), bf16[4,16,16,4352]{3,2,1,0:T(8,128)(2,1)}, u32[]{:S(2)}, u32[]{:S(2)}) async-start(bf16[4,16,16,4352]{3,2,1,0:T(8,128)(2,1)} %bitcast.256), calls=%async_computation.3 | async-start | bytes 17825792 | tf_op jit(solution)/shard_map/all_to_all | solution.py:76
  405.3 57.7 %copy-start.35 = (bf16[96,2048]{1,0:T(8,128)(2,1)S(1)}, bf16[96,2048]{1,0:T(8,128)(2,1)}, u32[]{:S(2)}) copy-start(bf16[96,2048]{1,0:T(8,128)(2,1)} %add_convert_fusion.2) | copy-start | bytes 1179652
  458.4 15.8 %all-to-all-start.2 = ((bf16[4,1,16,4352]{3,2,1,0:T(8,128)(2,1)}), bf16[4,1,16,4352]{3,2,1,0:T(8,128)(2,1)S(1)}, u32[]{:S(2)}, u32[]{:S(2)}) async-start(bf16[4,1,16,4352]{3,2,1,0:T(8,128)(2,1)} %bitcast.268), calls=%async_computation.2 | async-start | bytes 1114112 | tf_op jit(solution)/shard_map/all_to_all | solution.py:76
  474.2 21.8 %all-to-all-start.4 = ((bf16[4,4,16,4352]{3,2,1,0:T(8,128)(2,1)}), bf16[4,4,16,4352]{3,2,1,0:T(8,128)(2,1)}, u32[]{:S(2)}, u32[]{:S(2)}) async-start(bf16[4,4,16,4352]{3,2,1,0:T(8,128)(2,1)} %bitcast.261), calls=%async_computation.4 | async-start | bytes 4456448 | tf_op jit(solution)/shard_map/all_to_all | solution.py:76
  498.9 18.4 %copy-start.62 = (f32[96]{0:T(128)S(1)}, f32[96]{0:T(128)}, u32[]{:S(2)}) copy-start(f32[96]{0:T(128)} %get-tuple-element.82) | copy-start | bytes 1156
  498.9 18.4 %copy-start.26 = (bf16[1,96,1024]{2,1,0:T(8,128)(2,1)S(1)}, bf16[1,96,1024]{2,1,0:T(8,128)(2,1)}, u32[]{:S(2)}) copy-start(bf16[1,96,1024]{2,1,0:T(8,128)(2,1)} %param.15) | copy-start | bytes 589828
  498.9 18.4 %copy-start.40 = (f32[96,1024]{1,0:T(8,128)S(1)}, f32[96,1024]{1,0:T(8,128)}, u32[]{:S(2)}) copy-start(f32[96,1024]{1,0:T(8,128)} %get-tuple-element.188) | copy-start | bytes 1179652
  498.9 18.4 %copy-start.59 = (f32[96]{0:T(128)S(1)}, f32[96]{0:T(128)}, u32[]{:S(2)}) copy-start(f32[96]{0:T(128)} %copy-done.58) | copy-start | bytes 1156
  498.9 13.2 %all-to-all-start.5 = ((bf16[4,1,16,4352]{3,2,1,0:T(8,128)(2,1)}), bf16[4,1,16,4352]{3,2,1,0:T(8,128)(2,1)S(1)}, u32[]{:S(2)}, u32[]{:S(2)}) async-start(bf16[4,1,16,4352]{3,2,1,0:T(8,128)(2,1)} %bitcast.88), calls=%async_computation.5 | async-start | bytes 1114112 | tf_op jit(solution)/shard_map/all_to_all | solution.py:76
  517.3 3.6 collective-permute-start.14
  522.8 7.0 %copy-start.57 = (f32[8,3072]{1,0:T(8,128)}, f32[8,3072]{1,0:T(8,128)S(1)}, u32[]{:S(2)}) copy-start(f32[8,3072]{1,0:T(8,128)S(1)} %get-tuple-element.142) | copy-start | bytes 294916
  (44 other events, 115.1 us)
Sparse Core Ops, SparseCore 0:
  10.9 141.5 all-gather.6
